TPU v7x, 512 devices: a whole 4x8x8 slice. The times are simulated.
512 devices in a mesh: gx: 8 (over z), gy: 4 (over x), gz: 16 (over y, core).
Axes of the slice: x: 4, y: 8, z: 8, core: 2. Of those that a mesh axis runs over, the one named last changes fastest.
Arguments:
- body_forces: float32 [3, 64, 32, 2048], P(None, 'gx', 'gy', 'gz'), may hold values from -8 to 8, as said below
- material: int32 [64, 32, 2048], P('gx', 'gy', 'gz'), may hold values from 0 to 15
- fixed_mask: int32 [64, 32, 2048], P('gx', 'gy', 'gz'), may hold values 0 or 1
- moduli: float32 [2, 16], replicated, may hold values from 0.05 to 1
Outputs:
- displacement: float32 [3, 64, 32, 2048], P(None, 'gx', 'gy', 'gz')
- residual: float32 [3, 64, 32, 2048], P(None, 'gx', 'gy', 'gz')
Inputs may be any that keep to these rules, and one draw needn't show every extreme that they name: `body_forces`: forces on the voxels, of order one.
All inputs are finite; a program needn't handle non-finite values. No bound on the sum of `fixed_mask` on one device may be relied on, other than what follows from the above.
Results may differ from a plain program's by a relative error of at most 0.0001.
Values sent between devices are 32-bit elements; how exact they have to be, the bound alone decides.
No kernel may reach another device: no remote copies, remote signals or barrier semaphores. Data moves between devices by JAX's collectives and lax.ppermute only.
A program may use at most 128 MiB of HBM per device.

v0:
```python
import jax
import jax.numpy as jnp
from jax import lax
from jax.sharding import PartitionSpec as P

SMOOTH = 4
AGX = 1
AGY = 1
AGZ = 16
CLASSES = 16
CHEB_CENTER = 1.125
CHEB_HALF = 0.875


def with_halo(shard, sides, width):
    for axis, dim in sides:
        count, length = (lax.axis_size(axis), shard.shape[dim])
        up = [(i, (i + 1) % count) for i in range(count - 1)]
        down = [(j, i) for i, j in up]
        last = lax.slice_in_dim(shard, length - width, length, axis=dim)
        first = lax.slice_in_dim(shard, 0, width, axis=dim)
        before = lax.ppermute(last, axis, up)
        after = lax.ppermute(first, axis, down)
        shard = jnp.concatenate([before, shard, after], axis=dim)
    return shard


def coarsen(values, factor_x, factor_y, factor_z, method):
    leading = values.shape[:-3]
    size_x, size_y, size_z = values.shape[-3:]
    blocks = values.reshape(
        leading
        + (size_x // factor_x, factor_x, size_y // factor_y, factor_y, size_z // factor_z, factor_z)
    )
    offset = len(leading)
    summed_axes = (offset + 1, offset + 3, offset + 5)
    if method == "mean":
        return jnp.mean(blocks, axis=summed_axes)
    if method == "most":
        return jnp.max(blocks, axis=summed_axes)
    return jnp.sum(blocks, axis=summed_axes)


def prolong(values, factor_x, factor_y, factor_z):
    return jnp.repeat(
        jnp.repeat(jnp.repeat(values, factor_x, axis=-3), factor_y, axis=-2), factor_z, axis=-1
    )


def pad_zero(values):
    return jnp.pad(values, ((0, 0), (1, 1), (1, 1), (1, 1)))


def field_halo(values):
    return with_halo(values, (("gx", 1), ("gy", 2), ("gz", 3)), 1)


def material_halo(values):
    return with_halo(values, (("gx", 1), ("gy", 2), ("gz", 3)), 1)


def arrange(gathered, block_shape):
    count_x = lax.axis_size("gx")
    count_y = lax.axis_size("gy")
    count_z = lax.axis_size("gz")
    depth_dim, size_x, size_y, size_z = block_shape
    arranged = gathered.reshape((count_x, count_y, count_z, depth_dim, size_x, size_y, size_z))
    arranged = jnp.transpose(arranged, (3, 0, 4, 1, 5, 2, 6))
    return arranged.reshape((depth_dim, count_x * size_x, count_y * size_y, count_z * size_z))


def collect_material(block_values):
    gathered = lax.all_gather(block_values[None], ("gx", "gy", "gz"), axis=0, tiled=True)
    return arrange(gathered, block_values.shape)


def collect_residual(block_values):
    gathered = lax.all_gather(block_values[None], ("gx", "gy", "gz"), axis=0, tiled=True)
    return arrange(gathered, block_values.shape)


def own_block(whole_grid, block_shape):
    zero_start = jnp.zeros((), jnp.int32)
    start_x = lax.axis_index("gx") * block_shape[1]
    start_y = lax.axis_index("gy") * block_shape[2]
    start_z = lax.axis_index("gz") * block_shape[3]
    return lax.dynamic_slice(whole_grid, (zero_start, start_x, start_y, start_z), block_shape)


def prepare(material_now, active, scales, pad_material):
    padded = pad_material(material_now)
    face_vals = (
        0.5 * scales[0] * (padded[:, :-1, 1:-1, 1:-1] + padded[:, 1:, 1:-1, 1:-1]),
        0.5 * scales[1] * (padded[:, 1:-1, :-1, 1:-1] + padded[:, 1:-1, 1:, 1:-1]),
        0.5 * scales[2] * (padded[:, 1:-1, 1:-1, :-1] + padded[:, 1:-1, 1:-1, 1:]),
    )
    coefficients = []
    diagonals = []
    for component in range(3):
        stiff_row = []
        summed = jnp.zeros(active.shape, jnp.float32)
        for direction in range(3):
            facing = face_vals[direction]
            if component == direction:
                stiffness = facing[0] + (facing[1] + facing[0])
            else:
                stiffness = facing[0]
            length = active.shape[direction]
            summed = (
                summed
                + lax.slice_in_dim(stiffness, 0, length, axis=direction)
                + lax.slice_in_dim(stiffness, 1, length + 1, axis=direction)
            )
            stiff_row.append(stiffness)
        coefficients.append(stiff_row)
        diagonals.append(summed)
    diagonal = jnp.stack(diagonals)
    inverse = 1.0 / (active * diagonal + (1.0 - active))
    return (coefficients, diagonal, active, inverse)


def operate(values, level_data, pad_field):
    coefficients, diagonal, active, inverse = level_data
    masked = active * values
    padded = pad_field(masked)
    results = []
    for component in range(3):
        component_field = padded[component]
        summed = diagonal[component] * masked[component]
        neighbours = (
            (component_field[:-2, 1:-1, 1:-1], component_field[2:, 1:-1, 1:-1]),
            (component_field[1:-1, :-2, 1:-1], component_field[1:-1, 2:, 1:-1]),
            (component_field[1:-1, 1:-1, :-2], component_field[1:-1, 1:-1, 2:]),
        )
        for direction in range(3):
            stiffness = coefficients[component][direction]
            length = masked.shape[1 + direction]
            lower_faces = lax.slice_in_dim(stiffness, 0, length, axis=direction)
            upper_faces = lax.slice_in_dim(stiffness, 1, length + 1, axis=direction)
            summed = (
                summed
                - lower_faces * neighbours[direction][0]
                - upper_faces * neighbours[direction][1]
            )
        results.append(summed)
    return active * jnp.stack(results) + (1.0 - active) * values


def smooth(solution, residual, level_data, pad_field):
    inverse = level_data[3]
    center_ratio = CHEB_CENTER / CHEB_HALF
    rho_now = 1.0 / center_ratio
    update = inverse * residual / CHEB_CENTER
    for sweep_index in range(3):
        solution = solution + update
        residual = residual - operate(update, level_data, pad_field)
        if sweep_index < 2:
            rho_next = 1.0 / (2.0 * center_ratio - rho_now)
            update = rho_next * rho_now * update + 2.0 * rho_next / CHEB_HALF * inverse * residual
            rho_now = rho_next
    return (solution, residual)


def assemble(level_data):
    coefficients, diagonal, active, inverse = level_data
    grid_shape = active.shape
    cell_count = grid_shape[0] * grid_shape[1] * grid_shape[2]
    strides = (grid_shape[1] * grid_shape[2], grid_shape[2], 1)
    positions = jnp.arange(cell_count, dtype=jnp.int32)
    flat_active = active.reshape(cell_count)
    matrices = []
    for component in range(3):
        matrix = jnp.diag(diagonal[component].reshape(cell_count))
        for direction in range(3):
            length = grid_shape[direction]
            upper_faces = lax.slice_in_dim(
                coefficients[component][direction], 1, length + 1, axis=direction
            )
            inside = lax.broadcasted_iota(jnp.int32, grid_shape, direction) < length - 1
            link_values = jnp.where(inside, upper_faces, jnp.zeros_like(upper_faces)).reshape(
                cell_count
            )
            pattern = (positions[None, :] == positions[:, None] + strides[direction]).astype(
                jnp.float32
            )
            coupling = link_values[:, None] * pattern
            matrix = matrix - coupling - coupling.T
        matrix = flat_active[:, None] * matrix * flat_active[None, :] + jnp.diag(1.0 - flat_active)
        matrices.append(matrix)
    return jnp.stack(matrices)


def coarse_solve(factors, right_side):
    flat_side = right_side.reshape(3, -1)
    solved = jax.vmap(lambda factor, column: jax.scipy.linalg.cho_solve((factor, True), column))(
        factors, flat_side
    )
    return solved.reshape(right_side.shape)


def coarse_correction(factors, whole_residual):
    coarse_side = coarsen(whole_residual, AGX, AGY, AGZ, "sum")
    return prolong(coarse_solve(factors, coarse_side), AGX, AGY, AGZ)


def coarse_scales():
    extent_x = float(2 ** (SMOOTH - 1) * AGX)
    extent_y = float(2 ** (SMOOTH - 1) * AGY)
    extent_z = float(2 ** (SMOOTH - 1) * AGZ)
    return (
        extent_y * extent_z / extent_x,
        extent_x * extent_z / extent_y,
        extent_x * extent_y / extent_z,
    )


def descend(depth_now, right_side, level_list, finish):
    level_data = level_list[depth_now]
    solution, residual = smooth(jnp.zeros_like(right_side), right_side, level_data, field_halo)
    if depth_now + 1 < len(level_list):
        lower_solution = descend(
            depth_now + 1, coarsen(residual, 2, 2, 2, "sum"), level_list, finish
        )[0]
        correction = prolong(lower_solution, 2, 2, 2)
    else:
        correction = finish(residual)
    solution = solution + correction
    residual = residual - operate(correction, level_data, field_halo)
    return smooth(solution, residual, level_data, field_halo)


def body(body_forces, material, fixed_mask, moduli):
    class_ids = jnp.arange(CLASSES, dtype=jnp.int32)
    class_hits = material[None] == class_ids[:, None, None, None]
    shear_modulus = jnp.sum(jnp.where(class_hits, moduli[0][:, None, None, None], 0.0), axis=0)
    lame_modulus = jnp.sum(jnp.where(class_hits, moduli[1][:, None, None, None], 0.0), axis=0)
    materials = [jnp.stack([shear_modulus, lame_modulus])]
    actives = [(1 - fixed_mask).astype(jnp.float32)]
    for level_index in range(1, SMOOTH):
        materials.append(coarsen(materials[-1], 2, 2, 2, "mean"))
        actives.append(coarsen(actives[-1], 2, 2, 2, "most"))
    spread = SMOOTH
    base_level = min(spread, SMOOTH - 1)
    whole_stack = collect_material(
        jnp.concatenate([materials[base_level], actives[base_level][None]], axis=0)
    )
    whole_material = whole_stack[:2]
    whole_active = whole_stack[2]
    level_index = 3
    level_scale = float(2**level_index)
    coarse_level = prepare(
        coarsen(whole_material, AGX, AGY, AGZ, "mean"),
        coarsen(whole_active, AGX, AGY, AGZ, "most"),
        coarse_scales(),
        pad_zero,
    )
    factors = jnp.linalg.cholesky(assemble(coarse_level))

    def finish(residual):
        whole_rest = collect_residual(residual)
        return own_block(coarse_correction(factors, whole_rest), residual.shape)

    level_list = []
    for level_index in range(spread):
        level_scale = float(2**level_index)
        level_list.append(
            prepare(
                materials[level_index],
                actives[level_index],
                (level_scale, level_scale, level_scale),
                material_halo,
            )
        )
    displacement, residual = descend(0, body_forces, level_list, finish)
    return (displacement, residual)


def solution(mesh):
    return jax.shard_map(
        body,
        mesh=mesh,
        in_specs=(P(None, "gx", "gy", "gz"), P("gx", "gy", "gz"), P("gx", "gy", "gz"), P()),
        out_specs=(P(None, "gx", "gy", "gz"), P(None, "gx", "gy", "gz")),
        check_vma=False,
    )
```

profile of v0, /device:TPU:224, one launch (start us, length us, event | category | flops | bytes accessed | tf_op | source)
XLA Modules:
  0.0 1479.2 jit_solution(10990427274874191157)
XLA Ops:
  12.7 5.5 collective-permute-start.66
  20.7 5.1 collective-permute-start.18
  35.1 73.4 %all-gather = f32[1536,1,1,16]{3,2,1,0:T(1,128)S(1)} all-gather(f32[3,1,1,16]{3,2,1,0:T(1,128)S(1)} %copy.3022), channel_id=2, replica_groups=mesh['gx'=8,'gy'=4,'gz'=16] {'gx','gy','gz'}, dimensions={0}, use_global_device_ids=true | all-gather | bytes 98496 | tf_op jit(solution)/shard_map/all_gather | solution.py:73
  131.7 35.2 %custom-call.38 = f32[3,128,128]{2,1,0:T(8,128)S(1)} custom-call(f32[3,128,128]{2,1,0:T(8,128)S(1)} %cholesky.274), custom_call_target="Cholesky" | custom-call | tf_op jit(solution)/shard_map/jit(cholesky)/cholesky | solution.py:257
  168.0 30.9 %custom-call.39 = f32[3,1,128,128]{2,3,1,0:T(8,128)} custom-call(f32[3,1,128,128]{3,2,1,0:T(8,128)} %select_bitcast_fusion.2), custom_call_target="InvertDiagBlocksLowerTriangular" | custom-call | tf_op jit(solution)/shard_map/jit(cholesky)/cholesky | solution.py:257
  204.0 37.0 %custom-call.40 = f32[3,128,128]{2,1,0:T(8,128)} custom-call(f32[3,128,128]{2,1,0:T(8,128)} %cholesky.278), custom_call_target="Cholesky" | custom-call | tf_op jit(solution)/shard_map/jit(cholesky)/cholesky | solution.py:257
  242.6 30.9 %custom-call.41 = f32[3,1,128,128]{2,3,1,0:T(8,128)} custom-call(f32[3,1,128,128]{3,2,1,0:T(8,128)} %get-tuple-element.121), custom_call_target="InvertDiagBlocksLowerTriangular" | custom-call | tf_op jit(solution)/shard_map/jit(cholesky)/cholesky | solution.py:257
  278.4 36.6 %custom-call.42 = f32[3,128,128]{2,1,0:T(8,128)} custom-call(f32[3,128,128]{2,1,0:T(8,128)} %cholesky.283), custom_call_target="Cholesky" | custom-call | tf_op jit(solution)/shard_map/jit(cholesky)/cholesky | solution.py:257
  316.7 31.1 %custom-call.43 = f32[3,1,128,128]{2,3,1,0:T(8,128)} custom-call(f32[3,1,128,128]{3,2,1,0:T(8,128)} %get-tuple-element.119), custom_call_target="InvertDiagBlocksLowerTriangular" | custom-call | tf_op jit(solution)/shard_map/jit(cholesky)/cholesky | solution.py:257
  351.6 36.6 %custom-call.44 = f32[3,128,128]{2,1,0:T(8,128)} custom-call(f32[3,128,128]{2,1,0:T(8,128)} %convolution_subtract_fusion.2), custom_call_target="Cholesky" | custom-call | tf_op jit(solution)/shard_map/jit(cholesky)/cholesky | solution.py:257
  545.0 7.6 reshape.3725
  558.0 5.4 collective-permute-start.30
  583.4 5.4 collective-permute-start.36
  671.2 5.4 collective-permute-start.54
  764.2 5.4 collective-permute-start.78
  773.7 5.4 collective-permute-start.80
  780.3 13.6 while.1
  799.7 119.4 %custom-call.45 = f32[3,4,128,128]{2,3,1,0:T(8,128)} custom-call(f32[3,4,128,128]{3,2,1,0:T(8,128)} %bitcast.1520), custom_call_target="InvertDiagBlocksLowerTriangular" | custom-call | tf_op jit(solution)/shard_map/vmap(jit(_cho_solve))/triangular_solve | solution.py:195
  925.7 5.5 collective-permute-start.84
  958.4 5.2 collective-permute-start.90
  967.7 5.4 collective-permute-start.92
  988.2 82.1 %all_gather.7 = f32[512,3,1,1,16]{4,3,2,1,0:T(1,128)} all-gather(f32[1,3,1,1,16]{4,3,2,1,0:T(1,128)S(1)} %copy.3060), channel_id=1, replica_groups=mesh['gx'=8,'gy'=4,'gz'=16] {'gx','gy','gz'}, dimensions={0}, use_global_device_ids=true | all-gather | bytes 98496 | tf_op jit(solution)/shard_map/all_gather | solution.py:78
  1198.3 5.4 collective-permute-start.114
  1226.1 5.4 collective-permute-start.120
  1253.8 5.4 collective-permute-start.126
  1282.1 5.4 collective-permute-start.132
  1308.0 5.4 collective-permute-start.138
  1333.6 5.4 collective-permute-start.144
  1360.6 5.4 collective-permute-start.150
  1391.4 5.4 collective-permute-start.156
  1421.6 5.4 collective-permute-start.162
  1452.0 5.4 collective-permute-start.168
  (1151 shorter events, 844.1 us)
Async XLA Ops:
  10.8 384.2 %collective-permute-start.67 = (f32[2,1,1,16]{3,0,2,1:T(2,128)S(1)}, f32[2,1,1,16]{3,0,2,1:T(2,128)}, u32[]{:S(2)}, u32[]{:S(2)}) collective-permute-start(f32[2,1,1,16]{3,0,2,1:T(2,128)S(1)} %multiply_bitcast_fusion), channel_id=1, source_target_pairs={{64,0},{128,64},{192,128},{256,192},{320,256},{384,320},{448,384},... | collective-permute-start | bytes 392 | tf_op jit(solution)/shard_map/ppermute | solution.py:23
  12.7 385.4 %collective-permute-start.66 = (f32[2,1,1,16]{3,0,2,1:T(2,128)S(1)}, f32[2,1,1,16]{3,0,2,1:T(2,128)}, u32[]{:S(2)}, u32[]{:S(2)}) collective-permute-start(f32[2,1,1,16]{3,0,2,1:T(2,128)S(1)} %multiply_bitcast_fusion), channel_id=1, source_target_pairs={{0,64},{64,128},{128,192},{192,256},{256,320},{320,384},{384,448},... | collective-permute-start | bytes 392 | tf_op jit(solution)/shard_map/ppermute | solution.py:22
  18.8 397.2 %collective-permute-start.19 = (f32[2,1,4,64]{3,2,1,0:T(4,128)}, f32[2,1,4,64]{3,2,1,0:T(4,128)}, u32[]{:S(2)}, u32[]{:S(2)}) collective-permute-start(f32[2,1,4,64]{3,2,1,0:T(4,128)} %get-tuple-element.297), channel_id=1, source_target_pairs={{64,0},{128,64},{192,128},{256,192},{320,256},{384,320},{448,384},... | collective-permute-start | bytes 6152 | tf_op jit(solution)/shard_map/ppermute | solution.py:23
  20.7 400.4 %collective-permute-start.18 = (f32[2,1,4,64]{3,2,1,0:T(4,128)}, f32[2,1,4,64]{3,2,1,0:T(4,128)}, u32[]{:S(2)}, u32[]{:S(2)}) collective-permute-start(f32[2,1,4,64]{3,2,1,0:T(4,128)} %get-tuple-element.296), channel_id=1, source_target_pairs={{0,64},{64,128},{128,192},{192,256},{256,320},{320,384},{384,448},... | collective-permute-start | bytes 6152 | tf_op jit(solution)/shard_map/ppermute | solution.py:22
  26.5 405.0 %collective-permute-start.1 = (f32[2,1,8,128]{3,2,1,0:T(8,128)}, f32[2,1,8,128]{3,2,1,0:T(8,128)S(1)}, u32[]{:S(2)}, u32[]{:S(2)}) collective-permute-start(f32[2,1,8,128]{3,2,1,0:T(8,128)} %get-tuple-element.191), channel_id=1, source_target_pairs={{64,0},{128,64},{192,128},{256,192},{320,256},{384,320},{448,384},... | collective-permute-start | bytes 24584 | tf_op jit(solution)/shard_map/ppermute | solution.py:23
  394.9 9.7 collective-permute-start.43
  405.9 8.7 collective-permute-start.44
  410.6 21.0 %collective-permute-start = (f32[2,1,8,128]{3,2,1,0:T(8,128)S(1)}, f32[2,1,8,128]{3,2,1,0:T(8,128)S(1)}, u32[]{:S(2)}, u32[]{:S(2)}) collective-permute-start(f32[2,1,8,128]{3,2,1,0:T(8,128)S(1)} %copy-done.115), channel_id=1, source_target_pairs={{0,64},{64,128},{128,192},{192,256},{256,320},{320,384},{384,448},... | collective-permute-start | bytes 24584 | tf_op jit(solution)/shard_map/ppermute | solution.py:22
  414.7 262.0 %collective-permute-start.69 = (f32[2,3,1,16]{3,0,2,1:T(2,128)}, f32[2,3,1,16]{3,0,2,1:T(2,128)}, u32[]{:S(2)}, u32[]{:S(2)}) collective-permute-start(f32[2,3,1,16]{3,0,2,1:T(2,128)} %pad_maximum_fusion.148), channel_id=1, source_target_pairs={{16,0},{32,16},{48,32},{17,1},{33,17},{49,33},{18,2},{34,18},{50,3... | collective-permute-start | bytes 1160 | tf_op jit(solution)/shard_map/ppermute | solution.py:23
  416.0 260.6 %collective-permute-start.68 = (f32[2,3,1,16]{3,0,2,1:T(2,128)}, f32[2,3,1,16]{3,0,2,1:T(2,128)}, u32[]{:S(2)}, u32[]{:S(2)}) collective-permute-start(f32[2,3,1,16]{3,0,2,1:T(2,128)} %pad_maximum_fusion.148), channel_id=1, source_target_pairs={{0,16},{16,32},{32,48},{1,17},{17,33},{33,49},{2,18},{18,34},{34,5... | collective-permute-start | bytes 1160 | tf_op jit(solution)/shard_map/ppermute | solution.py:22
  470.0 8.3 collective-permute-start.10
  479.9 9.2 collective-permute-start.13
  482.0 11.9 collective-permute-start.12
  487.1 10.5 collective-permute-start.22
  489.1 8.6 collective-permute-start.23
  581.5 9.3 collective-permute-start.37
  583.4 9.8 collective-permute-start.36
  590.8 8.6 collective-permute-start.46
  620.3 13.8 collective-permute-start.51
  621.6 12.5 collective-permute-start.50
  634.9 15.8 %collective-permute-start.53 = (f32[3,6,6,1]{3,2,1,0:T(8,128)}, f32[3,6,6,1]{3,2,1,0:T(8,128)}, u32[]{:S(2)}, u32[]{:S(2)}) collective-permute-start(f32[3,6,6,1]{3,2,1,0:T(8,128)} %get-tuple-element.176), channel_id=1, source_target_pairs={{1,0},{2,1},{3,2},{4,3},{5,4},{6,5},{7,6},{8,7},{9,8},{10,9},{11,1... | collective-permute-start | bytes 1304 | tf_op jit(solution)/shard_map/ppermute | solution.py:23
  636.8 13.9 collective-permute-start.52
  697.7 11.4 collective-permute-start.61
  699.6 9.5 collective-permute-start.60
  704.8 17.1 %collective-permute-start.71 = (f32[2,3,3,1]{3,0,2,1:T(2,128)S(1)}, f32[2,3,3,1]{3,0,2,1:T(2,128)S(1)}, u32[]{:S(2)}, u32[]{:S(2)}) collective-permute-start(f32[2,3,3,1]{3,0,2,1:T(2,128)S(1)} %get-tuple-element.314), channel_id=1, source_target_pairs={{1,0},{2,1},{3,2},{4,3},{5,4},{6,5},{7,6},{8,7},{9,8},{10,9},{11,1... | collective-permute-start | bytes 224 | tf_op jit(solution)/shard_map/ppermute | solution.py:23
  706.7 15.2 %collective-permute-start.70 = (f32[2,3,3,1]{3,0,2,1:T(2,128)S(1)}, f32[2,3,3,1]{3,0,2,1:T(2,128)S(1)}, u32[]{:S(2)}, u32[]{:S(2)}) collective-permute-start(f32[2,3,3,1]{3,0,2,1:T(2,128)S(1)} %get-tuple-element.313), channel_id=1, source_target_pairs={{0,1},{1,2},{2,3},{3,4},{4,5},{5,6},{6,7},{7,8},{8,9},{9,10},{10,1... | collective-permute-start | bytes 224 | tf_op jit(solution)/shard_map/ppermute | solution.py:22
  772.4 21.5 %collective-permute-start.81 = (f32[3,3,1,16]{3,2,1,0:T(1,128)}, f32[3,3,1,16]{3,2,1,0:T(1,128)}, u32[]{:S(2)}, u32[]{:S(2)}) collective-permute-start(f32[3,3,1,16]{3,2,1,0:T(1,128)} %pad_maximum_fusion.130), channel_id=1, source_target_pairs={{16,0},{32,16},{48,32},{17,1},{33,17},{49,33},{18,2},{34,18},{50,3... | collective-permute-start | bytes 1736 | tf_op jit(solution)/shard_map/ppermute | solution.py:23
  773.7 20.2 %collective-permute-start.80 = (f32[3,3,1,16]{3,2,1,0:T(1,128)}, f32[3,3,1,16]{3,2,1,0:T(1,128)}, u32[]{:S(2)}, u32[]{:S(2)}) collective-permute-start(f32[3,3,1,16]{3,2,1,0:T(1,128)} %pad_maximum_fusion.130), channel_id=1, source_target_pairs={{0,16},{16,32},{32,48},{1,17},{17,33},{33,49},{2,18},{18,34},{34,5... | collective-permute-start | bytes 1736 | tf_op jit(solution)/shard_map/ppermute | solution.py:22
  795.3 123.7 %collective-permute-start.83 = (f32[3,3,3,1]{3,2,1,0:T(4,128)}, f32[3,3,3,1]{3,2,1,0:T(4,128)}, u32[]{:S(2)}, u32[]{:S(2)}) collective-permute-start(f32[3,3,3,1]{3,2,1,0:T(4,128)} %get-tuple-element.293), channel_id=1, source_target_pairs={{1,0},{2,1},{3,2},{4,3},{5,4},{6,5},{7,6},{8,7},{9,8},{10,9},{11,1... | collective-permute-start | bytes 332 | tf_op jit(solution)/shard_map/ppermute | solution.py:23
  797.3 121.8 %collective-permute-start.82 = (f32[3,3,3,1]{3,2,1,0:T(4,128)}, f32[3,3,3,1]{3,2,1,0:T(4,128)}, u32[]{:S(2)}, u32[]{:S(2)}) collective-permute-start(f32[3,3,3,1]{3,2,1,0:T(4,128)} %get-tuple-element.292), channel_id=1, source_target_pairs={{0,1},{1,2},{2,3},{3,4},{4,5},{5,6},{6,7},{7,8},{8,9},{9,10},{10,1... | collective-permute-start | bytes 332 | tf_op jit(solution)/shard_map/ppermute | solution.py:22
  1440.2 8.3 collective-permute-start.166
  1468.5 8.3 collective-permute-start.172
  (269 other events, 10081.9 us)
where the time goes:
time: 1490 us; the launch traced here: 1480 us
  starting transfers between devices  508 us (34%)
  other arithmetic  487 us (33%)
  waiting for transfers between devices  193 us (13%)
  blocking collectives  155 us (10%)
  local copies, waits for them, and re-layouts  104 us (7%)
  matrix products  25 us (2%)
    ppermute x87, starting transfers between devices, with_halo(): before = lax.ppermute(last, axis, up)  344 us
    another operation x18, other arithmetic, body(): factors = jnp.linalg.cholesky(assemble(coarse_level))  245 us
    ppermute x87, starting transfers between devices, with_halo(): after = lax.ppermute(first, axis, down)  164 us
    ppermute x87, waiting for transfers between devices, with_halo(): before = lax.ppermute(last, axis, up)  152 us
    another operation x15, other arithmetic, coarse_solve(): jax.scipy.linalg.cho_solve((factor, True), column)  132 us
    all_gather x1, blocking collectives, collect_residual(): lax.all_gather(block_values[None], ('gx', 'gy', 'gz'), axis=0, tiled=True)  82.1 us
    all_gather x1, blocking collectives, collect_material(): lax.all_gather(block_values[None], ('gx', 'gy', 'gz'), axis=0, tiled=True)  73.4 us
    ppermute x87, waiting for transfers between devices, with_halo(): after = lax.ppermute(first, axis, down)  40.9 us
  transfers between devices with their start and end apart: 174, of which 85 were waited for; matrix products, arithmetic and copies ran while one was open for 33% of the time, Pallas kernels for 0%

commit v1 on v0

--- a/solution.py
+++ b/solution.py
@@ -70,7 +70,15 @@
 
 
 def collect_material(block_values):
-    gathered = lax.all_gather(block_values[None], ("gx", "gy", "gz"), axis=0, tiled=True)
+    gathered = jnp.concatenate(
+        lax.all_to_all(
+            jnp.stack([block_values[None]] * lax.axis_size(("gx", "gy", "gz"))),
+            ("gx", "gy", "gz"),
+            0,
+            0,
+        ),
+        axis=0,
+    )
     return arrange(gathered, block_values.shape)
 
 

time: 1490 us -> 1350 us (0.906)
  blocking collectives: 155 us -> 75 us
  other arithmetic: 487 us -> 437 us
  local copies, waits for them, and re-layouts: 104 us -> 61.8 us
  starting transfers between devices: 508 us -> 529 us
    all_gather x1 -> x0, blocking collectives: 73.4 us -> none  [collect_material(): lax.all_gather(block_values[None], ('gx', 'gy', 'gz'), axis=0, tiled=True)]
    all_to_all x0 -> x1, starting transfers between devices: none -> 21.2 us  [collect_material(): lax.all_to_all(jnp.stack([block_values[None]] * lax.axis_size(('gx', 'gy'...]
    another operation x18, local copies, waits for them, and re-layouts: 23.5 us -> 3.83 us  [operate(): return active * jnp.stack(results) + (1.0 - active) * values]
  transfers between devices with their start and end apart: 174 -> 175, of which waited for: 85 -> 88; matrix products, arithmetic and copies ran while one was open for 33% -> 4% of each run, Pallas kernels for 0% -> 0%
where the time goes in v1:
time: 1350 us; the launch traced here: 1340 us
  starting transfers between devices  529 us (39%)
  other arithmetic  437 us (32%)
  waiting for transfers between devices  202 us (15%)
  blocking collectives  75 us (6%)
  local copies, waits for them, and re-layouts  61.8 us (5%)
  matrix products  22.6 us (2%)
    ppermute x87, starting transfers between devices, with_halo(): before = lax.ppermute(last, axis, up)  347 us
    another operation x18, other arithmetic, body(): factors = jnp.linalg.cholesky(assemble(coarse_level))  247 us
    ppermute x87, starting transfers between devices, with_halo(): after = lax.ppermute(first, axis, down)  161 us
    ppermute x87, waiting for transfers between devices, with_halo(): before = lax.ppermute(last, axis, up)  161 us
    another operation x15, other arithmetic, coarse_solve(): jax.scipy.linalg.cho_solve((factor, True), column)  125 us
    all_gather x1, blocking collectives, collect_residual(): lax.all_gather(block_values[None], ('gx', 'gy', 'gz'), axis=0, tiled=True)  75 us
    ppermute x87, waiting for transfers between devices, with_halo(): after = lax.ppermute(first, axis, down)  40.7 us
  transfers between devices with their start and end apart: 175, of which 88 were waited for; matrix products, arithmetic and copies ran while one was open for 4% of the time, Pallas kernels for 0%

profile of v1, /device:TPU:224, one launch (start us, length us, event | category | flops | bytes accessed | tf_op | source)
XLA Modules:
  0.0 1335.2 jit_solution(4993559770999551079)
XLA Ops:
  12.7 5.5 collective-permute-start.66
  29.4 21.2 %all-to-all-start = ((f32[512,1,3,1,1,16]{5,4,3,2,1,0:T(1,128)}), f32[512,1,3,1,1,16]{5,4,3,2,1,0:T(1,128)}, u32[]{:S(2)}, u32[]{:S(2)}) async-start(f32[512,1,3,1,1,16]{5,4,3,2,1,0:T(1,128)} %stack.514), calls=%async_computation | async-start | bytes 1572864 | tf_op jit(solution)/shard_map/all_to_all | solution.py:74
  113.5 5.1 collective-permute-start.6
  144.7 5.1 collective-permute-start.12
  207.8 7.6 reshape.3725
  220.7 5.4 collective-permute-start.30
  246.1 5.4 collective-permute-start.36
  306.7 5.4 collective-permute-start.54
  332.0 5.4 collective-permute-start.60
  389.0 5.4 collective-permute-start.78
  416.4 5.4 collective-permute-start.84
  444.4 5.4 collective-permute-start.90
  470.0 75.0 %all_gather.3 = f32[512,3,1,1,16]{4,3,2,1,0:T(1,128)S(1)} all-gather(f32[1,3,1,1,16]{4,3,2,1,0:T(1,128)S(1)} %copy.1409), channel_id=1, replica_groups=mesh['gx'=8,'gy'=4,'gz'=16] {'gx','gy','gz'}, dimensions={0}, use_global_device_ids=true | all-gather | bytes 98496 | tf_op jit(solution)/shard_map/all_gather | solution.py:86
  563.6 35.8 %custom-call.38 = f32[3,128,128]{2,1,0:T(8,128)} custom-call(f32[3,128,128]{2,1,0:T(8,128)S(1)} %cholesky.274), custom_call_target="Cholesky" | custom-call | tf_op jit(solution)/shard_map/jit(cholesky)/cholesky | solution.py:265
  602.3 30.9 %custom-call.39 = f32[3,1,128,128]{2,3,1,0:T(8,128)} custom-call(f32[3,1,128,128]{3,2,1,0:T(8,128)} %select_bitcast_fusion.2), custom_call_target="InvertDiagBlocksLowerTriangular" | custom-call | tf_op jit(solution)/shard_map/jit(cholesky)/cholesky | solution.py:265
  638.3 37.0 %custom-call.40 = f32[3,128,128]{2,1,0:T(8,128)} custom-call(f32[3,128,128]{2,1,0:T(8,128)} %cholesky.278), custom_call_target="Cholesky" | custom-call | tf_op jit(solution)/shard_map/jit(cholesky)/cholesky | solution.py:265
  676.9 30.9 %custom-call.41 = f32[3,1,128,128]{2,3,1,0:T(8,128)} custom-call(f32[3,1,128,128]{3,2,1,0:T(8,128)} %get-tuple-element.103), custom_call_target="InvertDiagBlocksLowerTriangular" | custom-call | tf_op jit(solution)/shard_map/jit(cholesky)/cholesky | solution.py:265
  712.7 36.6 %custom-call.42 = f32[3,128,128]{2,1,0:T(8,128)} custom-call(f32[3,128,128]{2,1,0:T(8,128)} %cholesky.283), custom_call_target="Cholesky" | custom-call | tf_op jit(solution)/shard_map/jit(cholesky)/cholesky | solution.py:265
  750.9 31.1 %custom-call.43 = f32[3,1,128,128]{2,3,1,0:T(8,128)} custom-call(f32[3,1,128,128]{3,2,1,0:T(8,128)} %get-tuple-element.101), custom_call_target="InvertDiagBlocksLowerTriangular" | custom-call | tf_op jit(solution)/shard_map/jit(cholesky)/cholesky | solution.py:265
  785.9 36.6 %custom-call.44 = f32[3,128,128]{2,1,0:T(8,128)} custom-call(f32[3,128,128]{2,1,0:T(8,128)} %convolution_subtract_fusion.2), custom_call_target="Cholesky" | custom-call | tf_op jit(solution)/shard_map/jit(cholesky)/cholesky | solution.py:265
  827.6 14.7 %while.1 = (s32[]{:T(128)}, f32[3,512,512]{2,1,0:T(8,128)}, s32[4,2]{0,1:T(2,128)S(1)}, f32[4,3,128,128]{3,2,0,1:T(8,128)}, s32[]{:T(128)}) while((s32[]{:T(128)}, f32[3,512,512]{2,1,0:T(8,128)}, s32[4,2]{0,1:T(2,128)S(1)}, f32[4,3,128,128]{3,2,0,1:T(8,128)}, s32[]{:T(128)}) %tuple.206), condition=%wide.while_cond, body=%wide.while_body.sunk | while | flops 2 | bytes 394349 | solution.py:203
  842.3 118.9 %custom-call.45 = f32[3,4,128,128]{2,3,1,0:T(8,128)S(1)} custom-call(f32[3,4,128,128]{3,2,1,0:T(8,128)} %bitcast.1530), custom_call_target="InvertDiagBlocksLowerTriangular" | custom-call | tf_op jit(solution)/shard_map/vmap(jit(_cho_solve))/triangular_solve | solution.py:203
  1060.4 5.4 collective-permute-start.114
  1086.1 5.4 collective-permute-start.120
  1111.7 5.4 collective-permute-start.126
  1137.9 5.4 collective-permute-start.132
  1163.7 5.4 collective-permute-start.138
  1189.4 5.4 collective-permute-start.144
  1216.3 5.4 collective-permute-start.150
  1247.1 5.4 collective-permute-start.156
  1277.4 5.4 collective-permute-start.162
  1307.8 5.4 collective-permute-start.168
  (1166 shorter events, 758.3 us)
Async XLA Ops:
  10.8 47.5 %collective-permute-start.67 = (f32[2,1,1,16]{3,0,2,1:T(2,128)S(1)}, f32[2,1,1,16]{3,0,2,1:T(2,128)S(1)}, u32[]{:S(2)}, u32[]{:S(2)}) collective-permute-start(f32[2,1,1,16]{3,0,2,1:T(2,128)S(1)} %multiply_bitcast_fusion), channel_id=1, source_target_pairs={{64,0},{128,64},{192,128},{256,192},{320,256},{384,320},{448,384},... | collective-permute-start | bytes 392 | tf_op jit(solution)/shard_map/ppermute | solution.py:23
  12.7 47.5 %collective-permute-start.66 = (f32[2,1,1,16]{3,0,2,1:T(2,128)S(1)}, f32[2,1,1,16]{3,0,2,1:T(2,128)S(1)}, u32[]{:S(2)}, u32[]{:S(2)}) collective-permute-start(f32[2,1,1,16]{3,0,2,1:T(2,128)S(1)} %multiply_bitcast_fusion), channel_id=1, source_target_pairs={{0,64},{64,128},{128,192},{192,256},{256,320},{320,384},{384,448},... | collective-permute-start | bytes 392 | tf_op jit(solution)/shard_map/ppermute | solution.py:22
  18.2 61.1 %collective-permute-start.19 = (f32[2,1,4,64]{3,2,1,0:T(4,128)S(1)}, f32[2,1,4,64]{3,2,1,0:T(4,128)S(1)}, u32[]{:S(2)}, u32[]{:S(2)}) collective-permute-start(f32[2,1,4,64]{3,2,1,0:T(4,128)S(1)} %get-tuple-element.277), channel_id=1, source_target_pairs={{64,0},{128,64},{192,128},{256,192},{320,256},{384,320},{448,384},... | collective-permute-start | bytes 6152 | tf_op jit(solution)/shard_map/ppermute | solution.py:23
  20.2 63.7 %collective-permute-start.18 = (f32[2,1,4,64]{3,2,1,0:T(4,128)S(1)}, f32[2,1,4,64]{3,2,1,0:T(4,128)S(1)}, u32[]{:S(2)}, u32[]{:S(2)}) collective-permute-start(f32[2,1,4,64]{3,2,1,0:T(4,128)S(1)} %get-tuple-element.276), channel_id=1, source_target_pairs={{0,64},{64,128},{128,192},{192,256},{256,320},{320,384},{384,448},... | collective-permute-start | bytes 6152 | tf_op jit(solution)/shard_map/ppermute | solution.py:22
  25.3 69.2 %collective-permute-start.1 = (f32[2,1,8,128]{3,2,1,0:T(8,128)S(1)}, f32[2,1,8,128]{3,2,1,0:T(8,128)S(1)}, u32[]{:S(2)}, u32[]{:S(2)}) collective-permute-start(f32[2,1,8,128]{3,2,1,0:T(8,128)S(1)} %get-tuple-element.173), channel_id=1, source_target_pairs={{64,0},{128,64},{192,128},{256,192},{320,256},{384,320},{448,384},... | collective-permute-start | bytes 24584 | tf_op jit(solution)/shard_map/ppermute | solution.py:23
  29.4 519.1 %all-to-all-start = ((f32[512,1,3,1,1,16]{5,4,3,2,1,0:T(1,128)}), f32[512,1,3,1,1,16]{5,4,3,2,1,0:T(1,128)}, u32[]{:S(2)}, u32[]{:S(2)}) async-start(f32[512,1,3,1,1,16]{5,4,3,2,1,0:T(1,128)} %stack.514), calls=%async_computation | async-start | bytes 1572864 | tf_op jit(solution)/shard_map/all_to_all | solution.py:74
  58.3 9.1 collective-permute-start.43
  68.7 9.3 collective-permute-start.44
  73.3 21.2 %collective-permute-start = (f32[2,1,8,128]{3,2,1,0:T(8,128)S(1)}, f32[2,1,8,128]{3,2,1,0:T(8,128)S(1)}, u32[]{:S(2)}, u32[]{:S(2)}) collective-permute-start(f32[2,1,8,128]{3,2,1,0:T(8,128)S(1)} %get-tuple-element.172), channel_id=1, source_target_pairs={{0,64},{64,128},{128,192},{192,256},{256,320},{320,384},{384,448},... | collective-permute-start | bytes 24584 | tf_op jit(solution)/shard_map/ppermute | solution.py:22
  78.0 234.1 %collective-permute-start.69 = (f32[2,3,1,16]{3,0,2,1:T(2,128)S(1)}, f32[2,3,1,16]{3,0,2,1:T(2,128)S(1)}, u32[]{:S(2)}, u32[]{:S(2)}) collective-permute-start(f32[2,3,1,16]{3,0,2,1:T(2,128)S(1)} %pad_maximum_fusion.148), channel_id=1, source_target_pairs={{16,0},{32,16},{48,32},{17,1},{33,17},{49,33},{18,2},{34,18},{50,3... | collective-permute-start | bytes 1160 | tf_op jit(solution)/shard_map/ppermute | solution.py:23
  79.3 232.8 %collective-permute-start.68 = (f32[2,3,1,16]{3,0,2,1:T(2,128)S(1)}, f32[2,3,1,16]{3,0,2,1:T(2,128)S(1)}, u32[]{:S(2)}, u32[]{:S(2)}) collective-permute-start(f32[2,3,1,16]{3,0,2,1:T(2,128)S(1)} %pad_maximum_fusion.148), channel_id=1, source_target_pairs={{0,16},{16,32},{32,48},{1,17},{17,33},{33,49},{2,18},{18,34},{34,5... | collective-permute-start | bytes 1160 | tf_op jit(solution)/shard_map/ppermute | solution.py:22
  132.8 8.3 collective-permute-start.10
  142.7 9.0 collective-permute-start.13
  144.7 12.0 collective-permute-start.12
  149.8 10.5 collective-permute-start.22
  151.7 8.6 collective-permute-start.23
  168.2 8.3 collective-permute-start.16
  197.7 8.3 collective-permute-start.28
  218.8 7.4 collective-permute-start.31
  244.1 9.3 collective-permute-start.37
  246.1 9.8 collective-permute-start.36
  253.4 8.6 collective-permute-start.46
  282.9 10.0 collective-permute-start.51
  284.2 8.7 collective-permute-start.50
  330.1 11.7 collective-permute-start.61
  332.0 9.8 collective-permute-start.60
  337.5 17.4 %collective-permute-start.71 = (f32[2,3,3,1]{3,0,2,1:T(2,128)S(1)}, f32[2,3,3,1]{3,0,2,1:T(2,128)S(1)}, u32[]{:S(2)}, u32[]{:S(2)}) collective-permute-start(f32[2,3,3,1]{3,0,2,1:T(2,128)S(1)} %get-tuple-element.294), channel_id=1, source_target_pairs={{1,0},{2,1},{3,2},{4,3},{5,4},{6,5},{7,6},{8,7},{9,8},{10,9},{11,1... | collective-permute-start | bytes 224 | tf_op jit(solution)/shard_map/ppermute | solution.py:23
  339.4 15.5 %collective-permute-start.70 = (f32[2,3,3,1]{3,0,2,1:T(2,128)S(1)}, f32[2,3,3,1]{3,0,2,1:T(2,128)S(1)}, u32[]{:S(2)}, u32[]{:S(2)}) collective-permute-start(f32[2,3,3,1]{3,0,2,1:T(2,128)S(1)} %get-tuple-element.293), channel_id=1, source_target_pairs={{0,1},{1,2},{2,3},{3,4},{4,5},{5,6},{6,7},{7,8},{8,9},{9,10},{10,1... | collective-permute-start | bytes 224 | tf_op jit(solution)/shard_map/ppermute | solution.py:22
  1235.1 8.3 collective-permute-start.154
  1265.7 8.3 collective-permute-start.160
  1295.9 8.3 collective-permute-start.166
  1324.3 8.3 collective-permute-start.172
  (284 other events, 14825.8 us)
